TPU v7x, 32 devices: a whole 2x2x4 slice. The times are simulated.
32 devices in a mesh: pix: 8 (over z, x), peak: 4 (over y, core).
Axes of the slice: x: 2, y: 2, z: 4, core: 2. Of those that a mesh axis runs over, the one named last changes fastest.
Arguments:
- cube: bfloat16 [32768, 8, 2048], P('pix', None, 'peak'), may hold values from -6 to 6
- pix_factor: bfloat16 [32768, 64], P(('pix', 'peak')), may hold values from -0.8984375 to 0.8984375
- sec_factor: bfloat16 [8, 64], replicated, may hold values from -5 to 5
- peak_factor: bfloat16 [2048, 64], P('peak'), may hold values from -0.046875 to 0.046875
Outputs:
- grad_pix: float32 [32768, 64], P(('pix', 'peak'))
- grad_peak: float32 [2048, 64], P('peak')
All inputs are finite; a program needn't handle non-finite values.
Results may differ from a plain program's by a relative error of at most 0.0003.
Values may be sent and summed in bfloat16 or wider, within the bound.
A program may use at most 128 MiB of HBM per device.

v0:
```python
import functools
import math

import jax
import jax.numpy as jnp
from jax import lax
from jax.experimental import pallas as pl
from jax.experimental.pallas import tpu as pltpu
from jax.sharding import PartitionSpec as P

MESH = pl.DeviceIdType.MESH
F32 = jnp.float32
BF16 = jnp.bfloat16
CHUNK = 256


def dot(a, b):
    return jnp.dot(a, b, preferred_element_type=F32)


def dot_nt(a, b):
    return lax.dot_general(a, b, (((1,), (1,)), ((), ())), preferred_element_type=F32)


def split3(x):
    one = x.astype(BF16)
    rest = x - one.astype(F32)
    two = rest.astype(BF16)
    return one, two, (rest - two.astype(F32)).astype(BF16)


def dot3(parts, b):
    return dot(parts[0], b) + (dot(parts[1], b) + dot(parts[2], b))


def kernel(
    n_pix, n_peak, per_block, scale,
    x_hbm, a_ref, b_ref, c_ref,
    gpix_ref, gpeak_ref,
    xbuf, at, spread, ab, wide, part, sib, far, gc, acc, pbuf, rbuf, cc, bt, ga, fix,
    x_sem, a_ssem, a_rsem, g_ssem, g_rsem, s_ssem, s_rsem, f_ssem, f_rsem,
    r_ssem, r_rsem, o_ssem, o_rsem,
):
    rank = c_ref.shape[0]
    sections = b_ref.shape[0]
    rows = CHUNK * sections
    half = CHUNK // 2
    n_chip = n_peak // 2
    wide_r = 2 * rank
    pix = lax.axis_index("pix")
    me = lax.axis_index("peak")
    chip = me // 2
    core = lax.rem(me, 2)
    sibling = 2 * chip + 1 - core
    own = n_peak - 1
    near = n_peak - 2

    blocks = []
    for d in range(1, n_chip):
        other = lax.rem(chip + d, n_chip)
        blocks += [2 * other + 1 - core, 2 * other + core]
    blocks += [sibling, me]

    pairs = [(d, k) for k in range(per_block) for d in range(1, n_chip)]
    early = pairs[:len(pairs) // 4], pairs[len(pairs) // 4:len(pairs) // 2]
    late = pairs[len(pairs) // 2:]

    def x_copy(pos, k):
        first = (blocks[pos] * per_block + k) * rows
        return pltpu.make_async_copy(
            x_hbm.at[pl.ds(pl.multiple_of(first, rows), rows), :],
            xbuf.at[pos * per_block + k],
            x_sem.at[pos * per_block + k],
        )

    def pair_x(d, k):
        return [x_copy(2 * (d - 1), k), x_copy(2 * (d - 1) + 1, k)]

    order = [c for p in early[0] for c in pair_x(*p)] + [x_copy(own, k) for k in range(per_block)]
    order += [c for p in early[1] for c in pair_x(*p)] + [x_copy(near, k) for k in range(per_block)]
    order += [c for p in late for c in pair_x(*p)]
    for copy in order:
        copy.start()

    barrier = pltpu.get_barrier_semaphore()
    for d in range(1, n_peak):
        pl.semaphore_signal(
            barrier, inc=1, device_id=(pix, lax.rem(me + d, n_peak)), device_id_type=MESH
        )
    for d in range(1, n_pix):
        pl.semaphore_signal(
            barrier, inc=1, device_id=(lax.rem(pix + d, n_pix), me), device_id_type=MESH
        )

    for k in range(per_block):
        at[own, k] = a_ref[:, k * CHUNK:(k + 1) * CHUNK]
    ct = c_ref[...].astype(F32)
    cc[...] = jnp.concatenate([ct, ct], axis=0).T.astype(BF16)
    gc[0] = dot(c_ref[...], cc[...])

    pl.semaphore_wait(barrier, n_peak - 1 + n_pix - 1)

    def a_send(index, src, dst, device):
        return pltpu.make_async_remote_copy(
            src_ref=at.at[src], dst_ref=at.at[dst],
            send_sem=a_ssem.at[index], recv_sem=a_rsem.at[dst],
            device_id=(pix, device), device_id_type=MESH,
        )

    a_out = []
    for d in range(1, n_chip):
        device = 2 * lax.rem(chip - d + n_chip, n_chip) + core
        a_out.append(a_send(2 * (d - 1), own, 2 * (d - 1) + 1, device))
        a_out[-1].start()
    a_out.append(a_send(near, own, near, sibling))
    a_out[-1].start()
    a_fwd = [
        a_send(2 * (d - 1) + 1, 2 * (d - 1) + 1, 2 * (d - 1), sibling) for d in range(1, n_chip)
    ]

    g_out = []
    for d in range(1, n_peak):
        g_out.append(pltpu.make_async_remote_copy(
            src_ref=gc.at[0], dst_ref=gc.at[d],
            send_sem=g_ssem.at[d - 1], recv_sem=g_rsem.at[d - 1],
            device_id=(pix, lax.rem(me + d, n_peak)), device_id_type=MESH,
        ))
        g_out[-1].start()

    row = lax.broadcasted_iota(jnp.int32, (rank, rank), 0)
    col = lax.broadcasted_iota(jnp.int32, (rank, rank), 1)
    eye = (row == col).astype(F32).astype(BF16)
    row = lax.broadcasted_iota(jnp.int32, (rank, wide_r), 0)
    col = lax.broadcasted_iota(jnp.int32, (rank, wide_r), 1)
    eye2 = ((row == col) | (row + rank == col)).astype(F32).astype(BF16)
    b_f = b_ref[...].astype(F32)
    b_tiled = jnp.broadcast_to(b_f[None], (CHUNK // sections, sections, rank))
    b_tiled = b_tiled.reshape(CHUNK, rank)
    bt[...] = dot_nt(eye, b_tiled.astype(BF16))
    bb = dot(b_ref[...], eye2)
    lead = lax.broadcasted_iota(jnp.int32, (CHUNK, rank), 0) < sections
    b_once = jnp.where(lead, b_tiled, 0.0).astype(BF16)
    gram_b = dot(dot_nt(eye, b_once).astype(BF16), b_once)
    row = lax.broadcasted_iota(jnp.int32, (CHUNK, CHUNK), 0)
    col = lax.broadcasted_iota(jnp.int32, (CHUNK, CHUNK), 1) // sections
    for j in range(sections):
        spread[j] = (row == col + j * (CHUNK // sections)).astype(F32).astype(BF16)
    ga[...] = jnp.zeros_like(ga)

    lane_lo = lax.broadcasted_iota(jnp.int32, (half * sections, wide_r), 1) < rank

    def pix_chunks(todo):
        for index, slot in todo:
            one = dot(xbuf[index, : half * sections, :], cc[...])
            two = dot(xbuf[index, half * sections:, :], cc[...])
            wide[slot] = jnp.where(lane_lo, one, two)
        for index, slot in todo:
            total = wide[slot, pl.ds(0, half, stride=sections), :] * bb[0:1, :]
            for s in range(1, sections):
                total += wide[slot, pl.ds(s, half, stride=sections), :] * bb[s:s + 1, :]
            part[index] = total

    def expand(pos):
        stacked = at[pos].reshape(per_block * rank, CHUNK)
        for j in range(sections):
            product = dot(stacked, spread[j]).reshape(per_block, rank, CHUNK) * bt[...][None]
            high = product.astype(BF16)
            low = (product - high.astype(F32)).astype(BF16)
            first = pos * per_block
            ab[first:first + per_block, :rank, j * CHUNK:(j + 1) * CHUNK] = high
            ab[first:first + per_block, rank:, j * CHUNK:(j + 1) * CHUNK] = low
        for k in range(per_block):
            ga[...] += dot_nt(at[pos, k], at[pos, k])

    def peak_mode(first, count, copy):
        step = 2 if count % 2 == 0 else 1

        def body(i, carry):
            if copy is not None:
                for k in range(step):
                    copy(i * step + k).wait()
            total = acc[...]
            for k in range(step):
                index = first + i * step + k
                total += dot(ab[index], xbuf[index])
            acc[...] = total
            return carry

        lax.fori_loop(0, count // step, body, 0)

    def sib_send(chip_slot, k):
        pos = 2 * chip_slot
        return pltpu.make_async_remote_copy(
            src_ref=part.at[pos * per_block + k], dst_ref=sib.at[chip_slot, k],
            send_sem=s_ssem.at[chip_slot, k], recv_sem=s_rsem.at[chip_slot, k],
            device_id=(pix, sibling), device_id_type=MESH,
        )

    def far_send(d, k):
        device = 2 * lax.rem(chip + d, n_chip) + core
        pos = 2 * (d - 1) + 1
        return pltpu.make_async_remote_copy(
            src_ref=part.at[pos * per_block + k], dst_ref=far.at[d - 1, k],
            send_sem=f_ssem.at[d - 1, k], recv_sem=f_rsem.at[d - 1, k],
            device_id=(pix, device), device_id_type=MESH,
        )

    def pair_mode(d, k):
        index = 2 * (d - 1) * per_block + k
        pix_chunks([(index, 0), (index + per_block, 1)])
        sib_send(d - 1, k).start()

    def pair_finish(d, k):
        sib_send(d - 1, k).wait_recv()
        part[(2 * (d - 1) + 1) * per_block + k] += sib[d - 1, k]
        far_send(d, k).start()

    acc[...] = jnp.zeros_like(acc)
    expand(own)
    for p in early[0]:
        for copy in pair_x(*p):
            copy.wait()
        pair_mode(*p)
    peak_mode(own * per_block, per_block, lambda k: x_copy(own, k))
    for p in early[0]:
        pair_finish(*p)
    a_out[-1].wait_recv()
    for p in early[1]:
        for copy in pair_x(*p):
            copy.wait()
    expand(near)
    for p in early[1]:
        pair_mode(*p)
    for d in range(1, n_chip):
        a_out[d - 1].wait_recv()
        a_fwd[d - 1].start()
    peak_mode(near * per_block, per_block, lambda k: x_copy(near, k))
    for p in early[1]:
        pair_finish(*p)
    for d in range(1, n_chip):
        a_fwd[d - 1].wait_recv()
    for pos in range(near):
        expand(pos)
    acc[:rank, :] -= dot3(split3(ga[...] * gram_b), c_ref[...])
    for p in late:
        for copy in pair_x(*p):
            copy.wait()
    peak_mode(0, near * per_block, None)

    pbuf[...] = ((acc[:rank, :] + acc[rank:, :]) * scale).reshape(pbuf.shape)
    r_out = []
    for d in range(1, n_pix):
        device = lax.rem(pix + d, n_pix)
        r_out.append(pltpu.make_async_remote_copy(
            src_ref=pbuf.at[device], dst_ref=rbuf.at[d - 1],
            send_sem=r_ssem.at[d - 1], recv_sem=r_rsem.at[d - 1],
            device_id=(device, me), device_id_type=MESH,
        ))
        r_out[-1].start()

    for n, p in enumerate(late):
        pair_mode(*p)
        if n > 0:
            pair_finish(*late[n - 1])

    def single_mode(pos, send):
        step = 2 if per_block % 2 == 0 else 1

        def body(i, carry):
            first = pos * per_block + i * step
            pix_chunks([(first + k, k) for k in range(step)])
            if send:
                for k in range(step):
                    sib_send(n_chip - 1, i * step + k).start()
            return carry

        lax.fori_loop(0, per_block // step, body, 0)

    for d in range(1, n_peak):
        g_out[d - 1].wait_recv()
    gram_c = gc[0]
    for d in range(1, n_peak):
        gram_c += gc[d]
    weight = split3(gram_b * gram_c[:, :rank])
    for k in range(per_block):
        fix[k] = dot3(weight, at[own, k])
    single_mode(near, True)
    for p in late[-1:]:
        pair_finish(*p)

    for d in range(1, n_pix):
        r_out[d - 1].wait_recv()
    total = pbuf[pix]
    for d in range(1, n_pix):
        total += rbuf[d - 1]
    gpeak_ref[pix] = total
    o_out = []
    for d in range(1, n_pix):
        device = lax.rem(pix + d, n_pix)
        o_out.append(pltpu.make_async_remote_copy(
            src_ref=gpeak_ref.at[pix], dst_ref=gpeak_ref.at[pix],
            send_sem=o_ssem.at[d - 1], recv_sem=o_rsem.at[d - 1],
            device_id=(device, me), device_id_type=MESH,
        ))
        o_out[-1].start()

    single_mode(own, False)

    for k in range(per_block):
        sib_send(n_chip - 1, k).wait_recv()
    for p in pairs:
        far_send(*p).wait_recv()
    for k in range(per_block):
        total = part[own * per_block + k] + sib[n_chip - 1, k]
        for d in range(1, n_chip):
            total += far[d - 1, k]
        total = total.T
        lo = k * CHUNK
        gpix_ref[:, lo:lo + half] = total[:rank] - fix[k, :, :half]
        gpix_ref[:, lo + half:lo + CHUNK] = total[rank:] - fix[k, :, half:]

    for d in range(1, n_pix):
        o_out[d - 1].wait_recv()
    for copy in a_out + a_fwd + g_out + r_out + o_out:
        copy.wait_send()
    for chip_slot in range(n_chip):
        for k in range(per_block):
            sib_send(chip_slot, k).wait_send()
    for p in pairs:
        far_send(*p).wait_send()


def place(pix_in, peak_in, pix_out, peak_out, sem):
    copies = [
        pltpu.make_async_copy(pix_in, pix_out, sem.at[0]),
        pltpu.make_async_copy(peak_in, peak_out, sem.at[1]),
    ]
    for copy in copies:
        copy.start()
    for copy in copies:
        copy.wait()


def solution(mesh):
    n_pix, n_peak = mesh.shape["pix"], mesh.shape["peak"]

    def on_device(cube, pix_factor, sec_factor, peak_factor):
        pixels, sections, peaks = cube.shape
        rank = peak_factor.shape[1]
        own = pix_factor.shape[0]
        per_block = own // CHUNK
        rows = CHUNK * sections
        n_chip = n_peak // 2
        n_far = max(n_chip - 1, 1)
        n_chunk = n_peak * per_block
        scale = 1.0 / math.sqrt(float(sections * pixels * n_pix))
        dma = pltpu.SemaphoreType.DMA
        vmem = pl.BlockSpec(memory_space=pltpu.VMEM)
        anywhere = pl.BlockSpec(memory_space=pl.ANY)
        packed = (CHUNK // 2, 2 * rank)
        grad_pix, grad_peak = pl.pallas_call(
            functools.partial(kernel, n_pix, n_peak, per_block, scale),
            out_shape=(
                jax.ShapeDtypeStruct((rank, own), F32),
                jax.ShapeDtypeStruct((n_pix, rank // n_pix, peaks), F32),
            ),
            in_specs=[anywhere, vmem, vmem, vmem],
            out_specs=(vmem, vmem),
            scratch_shapes=[
                pltpu.VMEM((n_chunk, rows, peaks), BF16),
                pltpu.VMEM((n_peak, per_block, rank, CHUNK), BF16),
                pltpu.VMEM((sections, CHUNK, CHUNK), BF16),
                pltpu.VMEM((n_chunk, 2 * rank, rows), BF16),
                pltpu.VMEM((2, rows // 2, 2 * rank), F32),
                pltpu.VMEM((n_chunk,) + packed, F32),
                pltpu.VMEM((n_chip, per_block) + packed, F32),
                pltpu.VMEM((n_far, per_block) + packed, F32),
                pltpu.VMEM((n_peak, rank, 2 * rank), F32),
                pltpu.VMEM((2 * rank, peaks), F32),
                pltpu.VMEM((n_pix, rank // n_pix, peaks), F32),
                pltpu.VMEM((n_pix - 1, rank // n_pix, peaks), F32),
                pltpu.VMEM((peaks, 2 * rank), BF16),
                pltpu.VMEM((rank, CHUNK), F32),
                pltpu.VMEM((rank, rank), F32),
                pltpu.VMEM((per_block, rank, CHUNK), F32),
                dma((n_chunk,)),
                dma((n_peak - 1,)), dma((n_peak - 1,)),
                dma((n_peak - 1,)), dma((n_peak - 1,)),
                dma((n_chip, per_block)), dma((n_chip, per_block)),
                dma((n_far, per_block)), dma((n_far, per_block)),
                dma((n_pix - 1,)), dma((n_pix - 1,)),
                dma((n_pix - 1,)), dma((n_pix - 1,)),
            ],
            compiler_params=pltpu.CompilerParams(
                collective_id=0, has_side_effects=True, vmem_limit_bytes=56 * 1024 * 1024
            ),
            name="cp_gradient",
        )(cube.reshape(pixels * sections, peaks), pix_factor.T, sec_factor, peak_factor.T)
        grad_pix, grad_peak = pl.pallas_call(
            place,
            out_shape=(
                jax.ShapeDtypeStruct((rank, own), F32),
                jax.ShapeDtypeStruct((rank, peaks), F32),
            ),
            in_specs=[pl.BlockSpec(memory_space=pltpu.HBM)] * 2,
            out_specs=(anywhere, anywhere),
            scratch_shapes=[dma((2,))],
            name="place_results",
        )(grad_pix, grad_peak.reshape(rank, peaks))
        return grad_pix.T, grad_peak.T

    in_specs = (P("pix", None, "peak"), P(("pix", "peak"), None), P(), P("peak", None))
    out_specs = (P(("pix", "peak"), None), P("peak", None))
    return jax.shard_map(
        on_device, mesh=mesh, in_specs=in_specs, out_specs=out_specs, check_vma=False
    )
```

profile of v0, /device:TPU:0, one launch (start us, length us, event | category | flops | bytes accessed | tf_op | source)
XLA Modules:
  0.0 43.2 jit_solution(12392849226419713199)
XLA Ops:
  0.6 29.5 %cp_gradient.1 = (f32[64,1024]{1,0:T(8,128)}, f32[8,8,512]{2,1,0:T(8,128)}) custom-call(bf16[32768,512]{1,0:T(8,128)(2,1)} %bitcast.6, bf16[64,1024]{1,0:T(8,128)(2,1)} %bitcast.7, bf16[8,64]{1,0:T(8,128)(2,1)} %b_ref.1, bf16[64,512]{1,0:T(8,128)(2,1)} %bitcast.9), custom_call_target="tpu_custom_call" | custom-call | tf_op jit(solution)/shard_map/cp_gradient/pallas_call | solution.py:361
  30.2 13.0 %place_results.1 = (f32[64,1024]{1,0:T(8,128)}, f32[64,512]{1,0:T(8,128)}) custom-call(f32[64,1024]{1,0:T(8,128)} %get-tuple-element.6.pix_in, f32[64,512]{1,0:T(8,128)} %bitcast.8), custom_call_target="tpu_custom_call" | custom-call | tf_op jit(solution)/shard_map/place_results/pallas_call | solution.py:399
where the time goes:
time: 43.4 us; the launch traced here: 43.2 us
  Pallas kernels  42.6 us (98%)
  between operations  0.64 us (1%)
    pallas_call x1, Pallas kernels, on_device(): pl.pallas_call(functools.partial(kernel, n_pix, n_peak, per_block, scale)...  29.5 us
    pallas_call x1, Pallas kernels, on_device(): pl.pallas_call(place, out_shape=(jax.ShapeDtypeStruct((rank, own), F32),...  13 us

commit v1 on v0

--- a/solution.py
+++ b/solution.py
@@ -62,8 +62,8 @@
     blocks += [sibling, me]
 
     pairs = [(d, k) for k in range(per_block) for d in range(1, n_chip)]
-    early = pairs[:len(pairs) // 4], pairs[len(pairs) // 4:len(pairs) // 2]
-    late = pairs[len(pairs) // 2:]
+    cuts = [len(pairs) * n // 4 for n in range(5)]
+    first, second, third, late = [pairs[lo:hi] for lo, hi in zip(cuts, cuts[1:])]
 
     def x_copy(pos, k):
         first = (blocks[pos] * per_block + k) * rows
@@ -76,9 +76,9 @@
     def pair_x(d, k):
         return [x_copy(2 * (d - 1), k), x_copy(2 * (d - 1) + 1, k)]
 
-    order = [c for p in early[0] for c in pair_x(*p)] + [x_copy(own, k) for k in range(per_block)]
-    order += [c for p in early[1] for c in pair_x(*p)] + [x_copy(near, k) for k in range(per_block)]
-    order += [c for p in late for c in pair_x(*p)]
+    order = [c for p in first for c in pair_x(*p)] + [x_copy(own, k) for k in range(per_block)]
+    order += [c for p in second for c in pair_x(*p)] + [x_copy(near, k) for k in range(per_block)]
+    order += [c for p in third + late for c in pair_x(*p)]
     for copy in order:
         copy.start()
 
@@ -188,6 +188,12 @@
 
         lax.fori_loop(0, count // step, body, 0)
 
+    def pair_peak(d, k):
+        index = 2 * (d - 1) * per_block + k
+        acc[...] += dot(ab[index], xbuf[index]) + dot(
+            ab[index + per_block], xbuf[index + per_block]
+        )
+
     def sib_send(chip_slot, k):
         pos = 2 * chip_slot
         return pltpu.make_async_remote_copy(
@@ -217,35 +223,42 @@
 
     acc[...] = jnp.zeros_like(acc)
     expand(own)
-    for p in early[0]:
+    for p in first:
         for copy in pair_x(*p):
             copy.wait()
         pair_mode(*p)
     peak_mode(own * per_block, per_block, lambda k: x_copy(own, k))
-    for p in early[0]:
+    for copy in a_out:
+        copy.wait_recv()
+    for copy in a_fwd:
+        copy.start()
+    for p in first:
         pair_finish(*p)
-    a_out[-1].wait_recv()
-    for p in early[1]:
+    for p in second:
         for copy in pair_x(*p):
             copy.wait()
     expand(near)
-    for p in early[1]:
+    for p in second:
         pair_mode(*p)
-    for d in range(1, n_chip):
-        a_out[d - 1].wait_recv()
-        a_fwd[d - 1].start()
-    peak_mode(near * per_block, per_block, lambda k: x_copy(near, k))
-    for p in early[1]:
-        pair_finish(*p)
-    for d in range(1, n_chip):
-        a_fwd[d - 1].wait_recv()
+    for copy in a_fwd:
+        copy.wait_recv()
     for pos in range(near):
         expand(pos)
+    for p in first + second:
+        pair_peak(*p)
+    for p in second:
+        pair_finish(*p)
     acc[:rank, :] -= dot3(split3(ga[...] * gram_b), c_ref[...])
+    peak_mode(near * per_block, per_block, lambda k: x_copy(near, k))
+    for p in third:
+        for copy in pair_x(*p):
+            copy.wait()
+        pair_mode(*p)
+        pair_peak(*p)
     for p in late:
         for copy in pair_x(*p):
             copy.wait()
-    peak_mode(0, near * per_block, None)
+        pair_peak(*p)
 
     pbuf[...] = ((acc[:rank, :] + acc[rank:, :]) * scale).reshape(pbuf.shape)
     r_out = []
@@ -258,10 +271,10 @@
         ))
         r_out[-1].start()
 
-    for n, p in enumerate(late):
+    for p in third:
+        pair_finish(*p)
+    for p in late:
         pair_mode(*p)
-        if n > 0:
-            pair_finish(*late[n - 1])
 
     def single_mode(pos, send):
         step = 2 if per_block % 2 == 0 else 1
@@ -285,7 +298,7 @@
     for k in range(per_block):
         fix[k] = dot3(weight, at[own, k])
     single_mode(near, True)
-    for p in late[-1:]:
+    for p in late:
         pair_finish(*p)
 
     for d in range(1, n_pix):
@@ -330,15 +343,9 @@
         far_send(*p).wait_send()
 
 
-def place(pix_in, peak_in, pix_out, peak_out, sem):
-    copies = [
-        pltpu.make_async_copy(pix_in, pix_out, sem.at[0]),
-        pltpu.make_async_copy(peak_in, peak_out, sem.at[1]),
-    ]
-    for copy in copies:
-        copy.start()
-    for copy in copies:
-        copy.wait()
+def place(pix_in, peak_in, pix_out, peak_out):
+    pix_out[...] = pix_in[...]
+    peak_out[...] = peak_in[...]
 
 
 def solution(mesh):
@@ -402,9 +409,8 @@
                 jax.ShapeDtypeStruct((rank, own), F32),
                 jax.ShapeDtypeStruct((rank, peaks), F32),
             ),
-            in_specs=[pl.BlockSpec(memory_space=pltpu.HBM)] * 2,
-            out_specs=(anywhere, anywhere),
-            scratch_shapes=[dma((2,))],
+            in_specs=[vmem, vmem],
+            out_specs=(vmem, vmem),
             name="place_results",
         )(grad_pix, grad_peak.reshape(rank, peaks))
         return grad_pix.T, grad_peak.T

time: 43.4 us -> 33.8 us (0.78)
  Pallas kernels: 42.6 us -> 33 us
    pallas_call x1, Pallas kernels: 13 us -> 1.74 us  [on_device(): pl.pallas_call(place, out_shape=(jax.ShapeDtypeStruct((rank, own), F32),...]
    pallas_call x1, Pallas kernels: 29.5 us -> 31.3 us  [on_device(): pl.pallas_call(functools.partial(kernel, n_pix, n_peak, per_block, scale)...]
where the time goes in v1:
time: 33.8 us; the launch traced here: 33.7 us
  Pallas kernels  33 us (98%)
  between operations  0.64 us (2%)
    pallas_call x1, Pallas kernels, on_device(): pl.pallas_call(functools.partial(kernel, n_pix, n_peak, per_block, scale)...  31.3 us
    pallas_call x1, Pallas kernels, on_device(): pl.pallas_call(place, out_shape=(jax.ShapeDtypeStruct((rank, own), F32),...  1.74 us

profile of v1, /device:TPU:0, one launch (start us, length us, event | category | flops | bytes accessed | tf_op | source)
XLA Modules:
  0.0 33.7 jit_solution(7189803495941402456)
XLA Ops:
  0.6 31.3 %cp_gradient.1 = (f32[64,1024]{1,0:T(8,128)}, f32[8,8,512]{2,1,0:T(8,128)}) custom-call(bf16[32768,512]{1,0:T(8,128)(2,1)} %bitcast.6, bf16[64,1024]{1,0:T(8,128)(2,1)} %bitcast.7, bf16[8,64]{1,0:T(8,128)(2,1)} %b_ref.1, bf16[64,512]{1,0:T(8,128)(2,1)} %bitcast.9), custom_call_target="tpu_custom_call" | custom-call | tf_op jit(solution)/shard_map/cp_gradient/pallas_call | solution.py:368
  31.9 1.7 %place_results.1 = (f32[64,1024]{1,0:T(8,128)}, f32[64,512]{1,0:T(8,128)}) custom-call(f32[64,1024]{1,0:T(8,128)} %get-tuple-element.6.pix_in, f32[64,512]{1,0:T(8,128)} %bitcast.8), custom_call_target="tpu_custom_call" | custom-call | tf_op jit(solution)/shard_map/place_results/pallas_call | solution.py:406

commit v2 on v1

--- a/solution.py
+++ b/solution.py
@@ -37,7 +37,7 @@
     n_pix, n_peak, per_block, scale,
     x_hbm, a_ref, b_ref, c_ref,
     gpix_ref, gpeak_ref,
-    xbuf, at, spread, ab, wide, part, sib, far, gc, acc, pbuf, rbuf, cc, bt, ga, fix,
+    xbuf, at, spread, ab, part, sib, far, gc, acc, pbuf, rbuf, cc, bt, ga, fix,
     x_sem, a_ssem, a_rsem, g_ssem, g_rsem, s_ssem, s_rsem, f_ssem, f_rsem,
     r_ssem, r_rsem, o_ssem, o_rsem,
 ):
@@ -148,17 +148,38 @@
     ga[...] = jnp.zeros_like(ga)
 
     lane_lo = lax.broadcasted_iota(jnp.int32, (half * sections, wide_r), 1) < rank
+    bb_all = jnp.broadcast_to(bb[None], (half, sections, wide_r))
+    sub = lax.broadcasted_iota(jnp.int32, (half // sections, sections, wide_r), 1)
+
+    def roll(x, shift):
+        return pltpu.roll(x, shift % sections, 1)
+
+    def section_sum(x):
+        level = [x[:, n] for n in range(sections)]
+        step = sections // 2
+        while step >= 1:
+            mask = lax.rem(sub, 2 * step) < step
+            pairs_of = list(zip(level[:step], level[step:]))
+            if 2 * step == sections:
+                level = [
+                    jnp.where(mask, one, two) + roll(jnp.where(mask, two, one), step)
+                    for one, two in pairs_of
+                ]
+            else:
+                level = [
+                    jnp.where(mask, one + roll(one, -step), two + roll(two, step))
+                    for one, two in pairs_of
+                ]
+            step //= 2
+        return level[0]
 
     def pix_chunks(todo):
-        for index, slot in todo:
-            one = dot(xbuf[index, : half * sections, :], cc[...])
-            two = dot(xbuf[index, half * sections:, :], cc[...])
-            wide[slot] = jnp.where(lane_lo, one, two)
-        for index, slot in todo:
-            total = wide[slot, pl.ds(0, half, stride=sections), :] * bb[0:1, :]
-            for s in range(1, sections):
-                total += wide[slot, pl.ds(s, half, stride=sections), :] * bb[s:s + 1, :]
-            part[index] = total
+        for index in todo:
+            full = dot(xbuf[index], cc[...])
+            both = jnp.where(lane_lo, full[: half * sections], full[half * sections:])
+            both = both.reshape(half, sections, wide_r) * bb_all
+            both = both.reshape(half // sections, sections, sections, wide_r)
+            part[index] = section_sum(both).reshape(half, wide_r)
 
     def expand(pos):
         stacked = at[pos].reshape(per_block * rank, CHUNK)
@@ -213,7 +234,7 @@
 
     def pair_mode(d, k):
         index = 2 * (d - 1) * per_block + k
-        pix_chunks([(index, 0), (index + per_block, 1)])
+        pix_chunks([index, index + per_block])
         sib_send(d - 1, k).start()
 
     def pair_finish(d, k):
@@ -281,7 +302,7 @@
 
         def body(i, carry):
             first = pos * per_block + i * step
-            pix_chunks([(first + k, k) for k in range(step)])
+            pix_chunks([first + k for k in range(step)])
             if send:
                 for k in range(step):
                     sib_send(n_chip - 1, i * step + k).start()
@@ -378,7 +399,6 @@
                 pltpu.VMEM((n_peak, per_block, rank, CHUNK), BF16),
                 pltpu.VMEM((sections, CHUNK, CHUNK), BF16),
                 pltpu.VMEM((n_chunk, 2 * rank, rows), BF16),
-                pltpu.VMEM((2, rows // 2, 2 * rank), F32),
                 pltpu.VMEM((n_chunk,) + packed, F32),
                 pltpu.VMEM((n_chip, per_block) + packed, F32),
                 pltpu.VMEM((n_far, per_block) + packed, F32),

time: 33.8 us -> 33.6 us (level)
  no operation moved by 1% of the time
where the time goes in v2:
time: 33.6 us; the launch traced here: 33.5 us
  Pallas kernels  32.9 us (98%)
  between operations  0.64 us (2%)
    pallas_call x1, Pallas kernels, on_device(): pl.pallas_call(functools.partial(kernel, n_pix, n_peak, per_block, scale)...  31.1 us
    pallas_call x1, Pallas kernels, on_device(): pl.pallas_call(place, out_shape=(jax.ShapeDtypeStruct((rank, own), F32),...  1.74 us

profile of v2, /device:TPU:0, one launch (start us, length us, event | category | flops | bytes accessed | tf_op | source)
XLA Modules:
  0.0 33.5 jit_solution(10021559702604614239)
XLA Ops:
  0.6 31.1 %cp_gradient.1 = (f32[64,1024]{1,0:T(8,128)}, f32[8,8,512]{2,1,0:T(8,128)}) custom-call(bf16[32768,512]{1,0:T(8,128)(2,1)} %bitcast.6, bf16[64,1024]{1,0:T(8,128)(2,1)} %bitcast.7, bf16[8,64]{1,0:T(8,128)(2,1)} %b_ref.1, bf16[64,512]{1,0:T(8,128)(2,1)} %bitcast.9), custom_call_target="tpu_custom_call" | custom-call | tf_op jit(solution)/shard_map/cp_gradient/pallas_call | solution.py:389
  31.7 1.7 %place_results.1 = (f32[64,1024]{1,0:T(8,128)}, f32[64,512]{1,0:T(8,128)}) custom-call(f32[64,1024]{1,0:T(8,128)} %get-tuple-element.6.pix_in, f32[64,512]{1,0:T(8,128)} %bitcast.8), custom_call_target="tpu_custom_call" | custom-call | tf_op jit(solution)/shard_map/place_results/pallas_call | solution.py:426

commit v3 on v2

--- a/solution.py
+++ b/solution.py
@@ -98,35 +98,6 @@
     cc[...] = jnp.concatenate([ct, ct], axis=0).T.astype(BF16)
     gc[0] = dot(c_ref[...], cc[...])
 
-    pl.semaphore_wait(barrier, n_peak - 1 + n_pix - 1)
-
-    def a_send(index, src, dst, device):
-        return pltpu.make_async_remote_copy(
-            src_ref=at.at[src], dst_ref=at.at[dst],
-            send_sem=a_ssem.at[index], recv_sem=a_rsem.at[dst],
-            device_id=(pix, device), device_id_type=MESH,
-        )
-
-    a_out = []
-    for d in range(1, n_chip):
-        device = 2 * lax.rem(chip - d + n_chip, n_chip) + core
-        a_out.append(a_send(2 * (d - 1), own, 2 * (d - 1) + 1, device))
-        a_out[-1].start()
-    a_out.append(a_send(near, own, near, sibling))
-    a_out[-1].start()
-    a_fwd = [
-        a_send(2 * (d - 1) + 1, 2 * (d - 1) + 1, 2 * (d - 1), sibling) for d in range(1, n_chip)
-    ]
-
-    g_out = []
-    for d in range(1, n_peak):
-        g_out.append(pltpu.make_async_remote_copy(
-            src_ref=gc.at[0], dst_ref=gc.at[d],
-            send_sem=g_ssem.at[d - 1], recv_sem=g_rsem.at[d - 1],
-            device_id=(pix, lax.rem(me + d, n_peak)), device_id_type=MESH,
-        ))
-        g_out[-1].start()
-
     row = lax.broadcasted_iota(jnp.int32, (rank, rank), 0)
     col = lax.broadcasted_iota(jnp.int32, (rank, rank), 1)
     eye = (row == col).astype(F32).astype(BF16)
@@ -244,6 +215,36 @@
 
     acc[...] = jnp.zeros_like(acc)
     expand(own)
+
+    pl.semaphore_wait(barrier, n_peak - 1 + n_pix - 1)
+
+    def a_send(index, src, dst, device):
+        return pltpu.make_async_remote_copy(
+            src_ref=at.at[src], dst_ref=at.at[dst],
+            send_sem=a_ssem.at[index], recv_sem=a_rsem.at[dst],
+            device_id=(pix, device), device_id_type=MESH,
+        )
+
+    a_out = []
+    for d in range(1, n_chip):
+        device = 2 * lax.rem(chip - d + n_chip, n_chip) + core
+        a_out.append(a_send(2 * (d - 1), own, 2 * (d - 1) + 1, device))
+        a_out[-1].start()
+    a_out.append(a_send(near, own, near, sibling))
+    a_out[-1].start()
+    a_fwd = [
+        a_send(2 * (d - 1) + 1, 2 * (d - 1) + 1, 2 * (d - 1), sibling) for d in range(1, n_chip)
+    ]
+
+    g_out = []
+    for d in range(1, n_peak):
+        g_out.append(pltpu.make_async_remote_copy(
+            src_ref=gc.at[0], dst_ref=gc.at[d],
+            send_sem=g_ssem.at[d - 1], recv_sem=g_rsem.at[d - 1],
+            device_id=(pix, lax.rem(me + d, n_peak)), device_id_type=MESH,
+        ))
+        g_out[-1].start()
+
     for p in first:
         for copy in pair_x(*p):
             copy.wait()
@@ -271,12 +272,7 @@
         pair_finish(*p)
     acc[:rank, :] -= dot3(split3(ga[...] * gram_b), c_ref[...])
     peak_mode(near * per_block, per_block, lambda k: x_copy(near, k))
-    for p in third:
-        for copy in pair_x(*p):
-            copy.wait()
-        pair_mode(*p)
-        pair_peak(*p)
-    for p in late:
+    for p in third + late:
         for copy in pair_x(*p):
             copy.wait()
         pair_peak(*p)
@@ -292,10 +288,10 @@
         ))
         r_out[-1].start()
 
-    for p in third:
-        pair_finish(*p)
-    for p in late:
+    for n, p in enumerate(third + late):
         pair_mode(*p)
+        if n > 0:
+            pair_finish(*(third + late)[n - 1])
 
     def single_mode(pos, send):
         step = 2 if per_block % 2 == 0 else 1
@@ -318,9 +314,9 @@
     weight = split3(gram_b * gram_c[:, :rank])
     for k in range(per_block):
         fix[k] = dot3(weight, at[own, k])
+    for p in late[-1:]:
+        pair_finish(*p)
     single_mode(near, True)
-    for p in late:
-        pair_finish(*p)
 
     for d in range(1, n_pix):
         r_out[d - 1].wait_recv()

time: 33.6 us -> 32.8 us (0.976)
  Pallas kernels: 32.9 us -> 32 us
    pallas_call x1, Pallas kernels: 31.1 us -> 30.3 us  [on_device(): pl.pallas_call(functools.partial(kernel, n_pix, n_peak, per_block, scale)...]
where the time goes in v3:
time: 32.8 us; the launch traced here: 32.6 us
  Pallas kernels  32 us (98%)
  between operations  0.64 us (2%)
    pallas_call x1, Pallas kernels, on_device(): pl.pallas_call(functools.partial(kernel, n_pix, n_peak, per_block, scale)...  30.3 us
    pallas_call x1, Pallas kernels, on_device(): pl.pallas_call(place, out_shape=(jax.ShapeDtypeStruct((rank, own), F32),...  1.74 us

profile of v3, /device:TPU:0, one launch (start us, length us, event | category | flops | bytes accessed | tf_op | source)
XLA Modules:
  0.0 32.6 jit_solution(351806914337111563)
XLA Ops:
  0.6 30.3 %cp_gradient.1 = (f32[64,1024]{1,0:T(8,128)}, f32[8,8,512]{2,1,0:T(8,128)}) custom-call(bf16[32768,512]{1,0:T(8,128)(2,1)} %bitcast.6, bf16[64,1024]{1,0:T(8,128)(2,1)} %bitcast.7, bf16[8,64]{1,0:T(8,128)(2,1)} %b_ref.1, bf16[64,512]{1,0:T(8,128)(2,1)} %bitcast.9), custom_call_target="tpu_custom_call" | custom-call | tf_op jit(solution)/shard_map/cp_gradient/pallas_call | solution.py:385
  30.9 1.7 %place_results.1 = (f32[64,1024]{1,0:T(8,128)}, f32[64,512]{1,0:T(8,128)}) custom-call(f32[64,1024]{1,0:T(8,128)} %get-tuple-element.6.pix_in, f32[64,512]{1,0:T(8,128)} %bitcast.8), custom_call_target="tpu_custom_call" | custom-call | tf_op jit(solution)/shard_map/place_results/pallas_call | solution.py:422

commit v4 on v3

--- a/solution.py
+++ b/solution.py
@@ -293,18 +293,17 @@
         if n > 0:
             pair_finish(*(third + late)[n - 1])
 
-    def single_mode(pos, send):
-        step = 2 if per_block % 2 == 0 else 1
+    def single_mode(pos, send, lo, hi):
+        step = 2 if lo % 2 == 0 and hi % 2 == 0 else 1
 
         def body(i, carry):
-            first = pos * per_block + i * step
-            pix_chunks([first + k for k in range(step)])
+            pix_chunks([pos * per_block + i * step + k for k in range(step)])
             if send:
                 for k in range(step):
                     sib_send(n_chip - 1, i * step + k).start()
             return carry
 
-        lax.fori_loop(0, per_block // step, body, 0)
+        lax.fori_loop(lo // step, hi // step, body, 0)
 
     for d in range(1, n_peak):
         g_out[d - 1].wait_recv()
@@ -316,7 +315,7 @@
         fix[k] = dot3(weight, at[own, k])
     for p in late[-1:]:
         pair_finish(*p)
-    single_mode(near, True)
+    single_mode(near, True, 0, per_block // 2)
 
     for d in range(1, n_pix):
         r_out[d - 1].wait_recv()
@@ -334,7 +333,8 @@
         ))
         o_out[-1].start()
 
-    single_mode(own, False)
+    single_mode(near, True, per_block // 2, per_block)
+    single_mode(own, False, 0, per_block)
 
     for k in range(per_block):
         sib_send(n_chip - 1, k).wait_recv()

time: 32.8 us -> 32.7 us (level)
  no operation moved by 1% of the time
where the time goes in v4:
time: 32.7 us; the launch traced here: 32.5 us
  Pallas kernels  31.9 us (98%)
  between operations  0.64 us (2%)
    pallas_call x1, Pallas kernels, on_device(): pl.pallas_call(functools.partial(kernel, n_pix, n_peak, per_block, scale)...  30.2 us
    pallas_call x1, Pallas kernels, on_device(): pl.pallas_call(place, out_shape=(jax.ShapeDtypeStruct((rank, own), F32),...  1.74 us

profile of v4, /device:TPU:0, one launch (start us, length us, event | category | flops | bytes accessed | tf_op | source)
XLA Modules:
  0.0 32.5 jit_solution(877922003633827875)
XLA Ops:
  0.6 30.2 %cp_gradient.1 = (f32[64,1024]{1,0:T(8,128)}, f32[8,8,512]{2,1,0:T(8,128)}) custom-call(bf16[32768,512]{1,0:T(8,128)(2,1)} %bitcast.6, bf16[64,1024]{1,0:T(8,128)(2,1)} %bitcast.7, bf16[8,64]{1,0:T(8,128)(2,1)} %b_ref.1, bf16[64,512]{1,0:T(8,128)(2,1)} %bitcast.9), custom_call_target="tpu_custom_call" | custom-call | tf_op jit(solution)/shard_map/cp_gradient/pallas_call | solution.py:385
  30.8 1.7 %place_results.1 = (f32[64,1024]{1,0:T(8,128)}, f32[64,512]{1,0:T(8,128)}) custom-call(f32[64,1024]{1,0:T(8,128)} %get-tuple-element.6.pix_in, f32[64,512]{1,0:T(8,128)} %bitcast.8), custom_call_target="tpu_custom_call" | custom-call | tf_op jit(solution)/shard_map/place_results/pallas_call | solution.py:422

commit v5 on v4

--- a/solution.py
+++ b/solution.py
@@ -294,7 +294,7 @@
             pair_finish(*(third + late)[n - 1])
 
     def single_mode(pos, send, lo, hi):
-        step = 2 if lo % 2 == 0 and hi % 2 == 0 else 1
+        step = math.gcd(math.gcd(lo, hi), 4)
 
         def body(i, carry):
             pix_chunks([pos * per_block + i * step + k for k in range(step)])

time: 32.7 us -> 32.7 us (level)
  no operation moved by 1% of the time
where the time goes in v5:
time: 32.7 us; the launch traced here: 32.5 us
  Pallas kernels  31.9 us (98%)
  between operations  0.64 us (2%)
    pallas_call x1, Pallas kernels, on_device(): pl.pallas_call(functools.partial(kernel, n_pix, n_peak, per_block, scale)...  30.2 us
    pallas_call x1, Pallas kernels, on_device(): pl.pallas_call(place, out_shape=(jax.ShapeDtypeStruct((rank, own), F32),...  1.74 us

profile of v5, /device:TPU:0, one launch (start us, length us, event | category | flops | bytes accessed | tf_op | source)
XLA Modules:
  0.0 32.5 jit_solution(10384590311081935266)
XLA Ops:
  0.6 30.2 %cp_gradient.1 = (f32[64,1024]{1,0:T(8,128)}, f32[8,8,512]{2,1,0:T(8,128)}) custom-call(bf16[32768,512]{1,0:T(8,128)(2,1)} %bitcast.6, bf16[64,1024]{1,0:T(8,128)(2,1)} %bitcast.7, bf16[8,64]{1,0:T(8,128)(2,1)} %b_ref.1, bf16[64,512]{1,0:T(8,128)(2,1)} %bitcast.9), custom_call_target="tpu_custom_call" | custom-call | tf_op jit(solution)/shard_map/cp_gradient/pallas_call | solution.py:385
  30.8 1.7 %place_results.1 = (f32[64,1024]{1,0:T(8,128)}, f32[64,512]{1,0:T(8,128)}) custom-call(f32[64,1024]{1,0:T(8,128)} %get-tuple-element.6.pix_in, f32[64,512]{1,0:T(8,128)} %bitcast.8), custom_call_target="tpu_custom_call" | custom-call | tf_op jit(solution)/shard_map/place_results/pallas_call | solution.py:422
